TPU v7x, 256 devices: a whole 4x4x8 slice. The times are simulated.
256 devices in a mesh: batch: 4 (over y_lo, core), seq: 64 (over z, x, y_hi).
Axes of the slice: x: 4, y: 4 (y_hi: 2, y_lo: 2; y = y_hi * 2 + y_lo), z: 8, core: 2. Of those that a mesh axis runs over, the one named last changes fastest.
Arguments:
- queries: bfloat16 [65536, 1024], P(('batch', 'seq')), parts along dimension 0, may hold values from -6 to 6
- keys: bfloat16 [65536, 1024], P(('batch', 'seq')), parts along dimension 0, may hold values from -6 to 6
- values: bfloat16 [65536, 1024], P(('batch', 'seq')), parts along dimension 0, may hold values from -6 to 6
- out_weight: bfloat16 [1024, 1024], replicated, may hold values from -0.1875 to 0.1875
Outputs:
- output: bfloat16 [65536, 1024], P(('batch', 'seq')), parts along dimension 0
There are 4 independent parts, one for each index of `batch`. A program takes and returns all parts, laid end to end along the dimension named above; an argument that names none is the same for every part. Nothing has to cross between parts.
All inputs are finite; a program needn't handle non-finite values.
Results may differ from a plain program's by a relative error of at most 0.011.
Values may be sent and summed in bfloat16 or wider, within the bound.
A program may use at most 64 MiB of HBM per device.

v0:
```python
import math

import jax
import jax.numpy as jnp
from jax import lax
from jax.experimental import pallas as pl
from jax.experimental.pallas import tpu as pltpu
from jax.sharding import PartitionSpec as P

MESH = pl.DeviceIdType.MESH
ROWS = 256
BLOCK = 128
D = 1024
HALF = 512
LANES = 128
CHUNKS = 4
FACTOR = math.log2(math.e) / 8.0
BF, F32 = jnp.bfloat16, jnp.float32
MASKED = -1e30


def averaging(rows):
    i = lax.broadcasted_iota(jnp.int32, (rows // 2, rows), 0)
    j = lax.broadcasted_iota(jnp.int32, (rows // 2, rows), 1)
    return jnp.where((j == 2 * i) | (j == 2 * i + 1), 0.5, 0.0).astype(BF)


def coarsen(x):
    rows = x.shape[0]
    if rows > 256:
        return jnp.concatenate([coarsen(x[i : i + 256]) for i in range(0, rows, 256)], axis=0)
    return jnp.dot(averaging(rows), x, preferred_element_type=F32).astype(BF)


def low_lanes(rows):
    return lax.broadcasted_iota(jnp.int32, (rows, LANES), 1) < 64


def split_keys(k):
    low, zero = low_lanes(k.shape[0]), jnp.zeros_like(k)
    return jnp.where(low, k, zero), jnp.where(low, zero, k)


def split_values(v):
    low, zero, one = low_lanes(v.shape[0]), jnp.zeros_like(v), jnp.ones_like(v)
    return (
        jnp.concatenate([jnp.where(low, v, zero), jnp.where(low, one, zero)], axis=1),
        jnp.concatenate([jnp.where(low, zero, v), jnp.where(low, zero, one)], axis=1),
    )


def attend(q, keys, values, masks=()):
    weights, peaks = [], []
    for k in keys:
        s = lax.dot_general(q, k, (((1,), (1,)), ((), ())), preferred_element_type=F32)
        for first, last, hidden in masks:
            parts = [s[:, :first], jnp.where(hidden, MASKED, s[:, first:last]), s[:, last:]]
            s = jnp.concatenate([part for part in parts if part.shape[1]], axis=1)
        peak = jnp.max(s, axis=1, keepdims=True)
        weights.append(jnp.exp2((s - peak) * FACTOR).astype(BF))
        peaks.append(peak * FACTOR)
    total = jnp.dot(
        jnp.concatenate(weights, axis=1), jnp.concatenate(values, axis=0), preferred_element_type=F32
    )
    peak = jnp.where(low_lanes(q.shape[0]), peaks[0], peaks[1])
    return peak, total[:, LANES:], total[:, :LANES]


def merge(a, b):
    peak = jnp.maximum(a[0], b[0])
    scale_a, scale_b = jnp.exp2(a[0] - peak), jnp.exp2(b[0] - peak)
    return peak, scale_a * a[1] + scale_b * b[1], scale_a * a[2] + scale_b * b[2]


def kernel(q_hbm, k_hbm, v_hbm, w_hbm, out_ref, *scratch):
    (own, qp, kx, vx, wv, st4, r4, z4s, z5s, z6s, z4r, z5r, z6r, cos, cor, s2, r2, s3, r3, ab, ret, acc, rep,
     own_sem, pair_sem, w_sem, e1s, e1r, nats, natr, rels, relr, s2s, s2r, s3s, s3r, a2as, a2ar, zs, zr, cs, cr,
     rs, rr, self_sem) = scratch
    b, s = lax.axis_index("batch"), lax.axis_index("seq")
    h, x, z, p = s % 2, (s // 2) % 4, s // 8, s // 2
    me8 = s % 8
    partner = (b, p * 2 + 1 - h)

    def pair(index):
        return (b, ((index + 32) % 32) * 2 + h)

    def in_plane(x2):
        return (b, z * 8 + x2 * 2 + h)

    def along_z(z2):
        return (b, z2 * 8 + me8)

    def flip(v, bits):
        for bit in (1, 2, 4):
            if bits & bit:
                v = v + bit - 2 * bit * ((v // bit) % 2)
        return v

    def remote(src, dst, ssem, rsem, target):
        return pltpu.make_async_remote_copy(
            src_ref=src, dst_ref=dst, send_sem=ssem, recv_sem=rsem, device_id=target, device_id_type=MESH
        )

    sent = []

    def send(*args):
        copy = remote(*args)
        copy.start()
        sent.append(copy)

    def received(dst, ssem, rsem):
        remote(dst, dst, ssem, rsem, partner).wait_recv()

    barrier = pltpu.get_barrier_semaphore()
    targets = [(b, z * 8 + (me8 + j) % 8) for j in range(1, 8)]
    targets += [along_z((z + j) % 8) for j in range(1, 8)]
    targets += [pair(p + 1), pair(p - 1)]
    for target in targets:
        pl.semaphore_signal(barrier, inc=1, device_id=target, device_id_type=MESH)

    inputs = (q_hbm, k_hbm, v_hbm)
    own_copies = [pltpu.make_async_copy(inputs[i], own.at[i], own_sem.at[i]) for i in range(3)]
    for copy in own_copies:
        copy.start()

    def mine(c):
        return pl.ds(pl.multiple_of(h * HALF + c * LANES, LANES), LANES)

    def theirs(c):
        return pl.ds(pl.multiple_of((1 - h) * HALF + c * LANES, LANES), LANES)

    def at(start, size):
        return pl.ds(pl.multiple_of(start, 128), size)

    pair_refs = (qp, kx, vx)
    offsets = (0, BLOCK, BLOCK)
    pair_copies = []
    for c in range(CHUNKS):
        for i in range(3):
            copy = pltpu.make_async_copy(
                inputs[i].at[:, mine(c)], pair_refs[i].at[c, at(offsets[i] + ROWS * h, ROWS)], pair_sem.at[c, i]
            )
            copy.start()
            pair_copies.append(copy)
    w_copy = pltpu.make_async_copy(w_hbm, wv, w_sem)
    w_copy.start()

    for i in range(3):
        own_copies[i].wait()
        coarse = own[i]
        for _ in range(4):
            coarse = coarsen(coarse)
        for hp in range(8):
            st4[(hp % 4) * 2 + hp // 4, i] = coarse[:, hp * LANES : (hp + 1) * LANES]

    pl.semaphore_wait(barrier, len(targets))

    for j in range(1, 8):
        t = (me8 + j) % 8
        send(st4.at[t], r4.at[:, pl.ds(pl.multiple_of(me8 * 16, 16), 16)], a2as.at[t], a2ar.at[me8], (b, z * 8 + t))
    self_copy = pltpu.make_async_copy(st4.at[me8], r4.at[:, pl.ds(pl.multiple_of(me8 * 16, 16), 16)], self_sem)
    self_copy.start()

    def exchange(c, i):
        send(
            inputs[i].at[:, theirs(c)],
            pair_refs[i].at[c, at(offsets[i] + ROWS * h, ROWS)],
            e1s.at[c, i],
            e1r.at[c, i],
            partner,
        )

    def exchanged(c, i):
        received(pair_refs[i].at[c, at(offsets[i] + ROWS * (1 - h), ROWS)], e1s.at[c, i], e1r.at[c, i])

    for c, i in ((0, 1), (0, 2), (1, 1), (1, 2), (0, 0), (2, 1), (2, 2), (1, 0), (3, 1), (3, 2), (2, 0), (3, 0)):
        exchange(c, i)

    native_target = pair(p - 1 + 2 * h)
    relay_target = pair(p + 1 - 2 * h)
    for c in range(CHUNKS):
        for i in (1, 2):
            send(
                inputs[i].at[at(BLOCK * h, BLOCK), mine(c)],
                pair_refs[i].at[c, at(640 * (1 - h), BLOCK)],
                nats.at[c, i - 1],
                natr.at[c, i - 1],
                native_target,
            )

    def spread(c):
        for i in (1, 2):
            pair_copies[c * 3 + i].wait()
            exchanged(c, i)
            send(
                pair_refs[i].at[c, at(BLOCK * (4 - 3 * h), BLOCK)],
                pair_refs[i].at[c, at(640 * h, BLOCK)],
                rels.at[c, i - 1],
                relr.at[c, i - 1],
                relay_target,
            )
            level2 = coarsen(coarsen(pair_refs[i][c, BLOCK : BLOCK + 512]))
            s2[c, i - 1] = level2
            s3[c, i - 1] = coarsen(level2)
        send(s2.at[c], r2.at[c], s2s.at[c], s2r.at[c], in_plane(flip(x, 1)))
        for k in (0, 1):
            send(
                s3.at[c], r3.at[c, :, pl.ds(64 * k, 64)], s3s.at[c, k], s3r.at[c, k], in_plane(flip(x, 2 + k))
            )

    def coarse_spread():
        self_copy.wait()
        for j in range(1, 8):
            t = (me8 + j) % 8
            received(r4.at[:, pl.ds(pl.multiple_of(t * 16, 16), 16)], a2as.at[t], a2ar.at[t])
        for i in (1, 2):
            level4 = r4[i]
            level5 = coarsen(level4)
            z4s[i - 1] = level4
            z5s[i - 1] = level5
            z6s[i - 1] = coarsen(level5)
        send(z4s, z4r, zs.at[0], zr.at[0], along_z(flip(z, 1)))
        for k in range(2):
            send(z5s, z5r.at[:, pl.ds(64 * k, 64)], zs.at[1 + k], zr.at[1 + k], along_z(flip(z, 2 + k)))
        for k in range(4):
            send(z6s, z6r.at[:, pl.ds(32 * k, 32)], zs.at[3 + k], zr.at[3 + k], along_z(flip(z, 4 + k)))

    def repeated(level):
        rows = level[0].shape[0]
        for i in range(3):
            rep[i, pl.ds(0, rows, stride=2), :] = level[i]
            rep[i, pl.ds(1, rows, stride=2), :] = level[i]
        return tuple(rep[i, : 2 * rows, :] for i in range(3))

    def coarse_attend():
        received(z4r, zs.at[0], zr.at[0])
        for k in range(2):
            received(z5r.at[:, pl.ds(64 * k, 64)], zs.at[1 + k], zr.at[1 + k])
        for k in range(4):
            received(z6r.at[:, pl.ds(32 * k, 32)], zs.at[3 + k], zr.at[3 + k])
        q4 = r4[0]
        q5 = coarsen(q4)
        q6 = coarsen(q5)
        level = attend(q6, split_keys(z6r[0]), split_values(z6r[1]))
        level = merge(repeated(level), attend(q5, split_keys(z5r[0]), split_values(z5r[1])))
        level = merge(repeated(level), attend(q4, split_keys(z4r[0]), split_values(z4r[1])))
        for i in range(3):
            for x2 in range(4):
                cos[x2, i] = level[i][x2 * 32 : x2 * 32 + 32]
        for j in range(1, 4):
            x2 = (x + j) % 4
            send(cos.at[x2], cor.at[x], cs.at[x2], cr.at[x], in_plane(x2))
        local = pltpu.make_async_copy(cos.at[x], cor.at[x], self_sem)
        local.start()
        local.wait()

    def coarse_received():
        for j in range(1, 4):
            x2 = (x + j) % 4
            received(cor.at[x2], cs.at[x2], cr.at[x2])

    def compute(c):
        pair_copies[c * 3].wait()
        exchanged(c, 0)
        q0 = qp[c]
        q1 = coarsen(q0)
        q2 = coarsen(q1)
        q3 = coarsen(q2)
        for k in (0, 1):
            received(r3.at[c, :, pl.ds(64 * k, 64)], s3s.at[c, k], s3r.at[c, k])
        level = tuple(cor[c, i] for i in range(3))
        level = merge(repeated(level), attend(q3, split_keys(r3[c, 0]), split_values(r3[c, 1])))
        received(r2.at[c], s2s.at[c], s2r.at[c])
        level = merge(repeated(level), attend(q2, split_keys(r2[c, 0]), split_values(r2[c, 1])))
        k1 = split_keys(coarsen(kx[c, BLOCK : BLOCK + 512]))
        v1 = split_values(coarsen(vx[c, BLOCK : BLOCK + 512]))
        parts = []
        for block in (0, 1):
            other = slice(128 * (1 - block), 128 * (2 - block))
            parts.append(attend(q1[128 * block : 128 * block + 128], [k[other] for k in k1], [v[other] for v in v1]))
        fine = tuple(jnp.concatenate([part[i] for part in parts], axis=0) for i in range(3))
        level = repeated(merge(repeated(level), fine))
        for i in (1, 2):
            received(pair_refs[i].at[c, at(640 * (1 - h), BLOCK)], nats.at[c, i - 1], natr.at[c, i - 1])
            received(pair_refs[i].at[c, at(640 * h, BLOCK)], rels.at[c, i - 1], relr.at[c, i - 1])
        k0 = split_keys(kx[c])
        v0 = split_values(vx[c])
        for block in range(4):
            window = slice(128 * block, 128 * block + 384)
            rows = slice(128 * block, 128 * block + 128)
            masks = ()
            if block == 0:
                masks = ((0, 128, p == 0),)
            if block == 3:
                masks = ((256, 384, p == 31),)
            fine = attend(q0[rows], [k[window] for k in k0], [v[window] for v in v0], masks)
            _, mass, summary = merge(tuple(a[rows] for a in level), fine)
            ab[c, rows] = (summary / mass).astype(BF)
        send(ab.at[c, at(ROWS * (1 - h), ROWS)], ret.at[c], rs.at[c], rr.at[c], partner)

    spread(0)
    coarse_spread()
    spread(1)
    coarse_attend()
    spread(2)
    coarse_received()
    compute(0)
    spread(3)
    compute(1)
    compute(2)
    compute(3)

    w_copy.wait()
    for c in range(CHUNKS):
        part = jnp.dot(
            ab[c, at(ROWS * h, ROWS)], wv[at(HALF * h + LANES * c, LANES)], preferred_element_type=F32
        )
        if c == 0:
            acc[...] = part
        else:
            acc[...] += part
    for c in range(CHUNKS):
        received(ret.at[c], rs.at[c], rr.at[c])
        part = jnp.dot(ret[c], wv[at(HALF * (1 - h) + LANES * c, LANES)], preferred_element_type=F32)
        if c < CHUNKS - 1:
            acc[...] += part
        else:
            out_ref[...] = (acc[...] + part).astype(BF)
    for copy in sent:
        copy.wait_send()


def local(queries, keys, values, out_weight):
    vmem = pltpu.VMEM
    dma = pltpu.SemaphoreType.DMA
    scratch = [
        vmem((3, ROWS, D), BF),
        vmem((CHUNKS, 512, LANES), BF),
        vmem((CHUNKS, 768, LANES), BF),
        vmem((CHUNKS, 768, LANES), BF),
        vmem((D, D), BF),
        vmem((8, 3, 16, LANES), BF),
        vmem((3, 128, LANES), BF),
        vmem((2, 128, LANES), BF),
        vmem((2, 64, LANES), BF),
        vmem((2, 32, LANES), BF),
        vmem((2, 128, LANES), BF),
        vmem((2, 128, LANES), BF),
        vmem((2, 128, LANES), BF),
        vmem((4, 3, 32, LANES), F32),
        vmem((4, 3, 32, LANES), F32),
        vmem((CHUNKS, 2, 128, LANES), BF),
        vmem((CHUNKS, 2, 128, LANES), BF),
        vmem((CHUNKS, 2, 64, LANES), BF),
        vmem((CHUNKS, 2, 128, LANES), BF),
        vmem((CHUNKS, 512, LANES), BF),
        vmem((CHUNKS, ROWS, LANES), BF),
        vmem((ROWS, D), F32),
        vmem((3, 512, LANES), F32),
        dma((3,)),
        dma((CHUNKS, 3)),
        dma,
        dma((CHUNKS, 3)),
        dma((CHUNKS, 3)),
        dma((CHUNKS, 2)),
        dma((CHUNKS, 2)),
        dma((CHUNKS, 2)),
        dma((CHUNKS, 2)),
        dma((CHUNKS,)),
        dma((CHUNKS,)),
        dma((CHUNKS, 2)),
        dma((CHUNKS, 2)),
        dma((8,)),
        dma((8,)),
        dma((7,)),
        dma((7,)),
        dma((4,)),
        dma((4,)),
        dma((CHUNKS,)),
        dma((CHUNKS,)),
        dma,
    ]
    anywhere = pl.BlockSpec(memory_space=pl.ANY)
    return pl.pallas_call(
        kernel,
        out_shape=jax.ShapeDtypeStruct((ROWS, D), BF),
        in_specs=[anywhere] * 4,
        out_specs=pl.BlockSpec(memory_space=pltpu.VMEM),
        scratch_shapes=scratch,
        compiler_params=pltpu.CompilerParams(
            collective_id=0, has_side_effects=True, vmem_limit_bytes=40 << 20
        ),
        cost_estimate=pl.CostEstimate(flops=1 << 30, bytes_accessed=4 << 20, transcendentals=1 << 21),
    )(queries, keys, values, out_weight)


def solution(mesh):
    rows = P(("batch", "seq"), None)
    return jax.shard_map(
        local, mesh=mesh, in_specs=(rows, rows, rows, P()), out_specs=rows, check_vma=False
    )
```

profile of v0, /device:TPU:2, one launch (start us, length us, event | category | flops | bytes accessed | tf_op | source)
XLA Modules:
  0.0 56.3 jit_solution(16575324542171110796)
XLA Ops:
  0.0 0.0 copy-start
  0.0 1.6 %copy-done = bf16[1024,1024]{1,0:T(8,128)(2,1)S(1)} copy-done((bf16[1024,1024]{1,0:T(8,128)(2,1)S(1)}, bf16[1024,1024]{1,0:T(8,128)(2,1)}, u32[]{:S(2)}) %copy-start) | copy-done | bytes 2097176
  1.6 0.0 copy-start.1
  1.6 1.0 %copy-done.1 = bf16[256,1024]{1,0:T(8,128)(2,1)S(1)} copy-done((bf16[256,1024]{1,0:T(8,128)(2,1)S(1)}, bf16[256,1024]{1,0:T(8,128)(2,1)}, u32[]{:S(2)}) %copy-start.1) | copy-done | bytes 524312
  2.6 0.0 copy-start.2
  2.6 1.0 %copy-done.2 = bf16[256,1024]{1,0:T(8,128)(2,1)S(1)} copy-done((bf16[256,1024]{1,0:T(8,128)(2,1)S(1)}, bf16[256,1024]{1,0:T(8,128)(2,1)}, u32[]{:S(2)}) %copy-start.2) | copy-done | bytes 524312
  3.7 0.0 copy-start.3
  3.7 1.0 %copy-done.3 = bf16[256,1024]{1,0:T(8,128)(2,1)S(1)} copy-done((bf16[256,1024]{1,0:T(8,128)(2,1)S(1)}, bf16[256,1024]{1,0:T(8,128)(2,1)}, u32[]{:S(2)}) %copy-start.3) | copy-done | bytes 524312
  4.7 50.8 %shard_map.46 = bf16[256,1024]{1,0:T(8,128)(2,1)S(1)} custom-call(bf16[256,1024]{1,0:T(8,128)(2,1)S(1)} %copy-done.1, bf16[256,1024]{1,0:T(8,128)(2,1)S(1)} %copy-done.2, bf16[256,1024]{1,0:T(8,128)(2,1)S(1)} %copy-done.3, bf16[1024,1024]{1,0:T(8,128)(2,1)S(1)} %copy-done), custom_call_target="tpu_custom_call" | custom-call | flops 1073741824 | bytes 4194304 | tf_op jit(solution)/shard_map/pallas_call | solution.py:384
  55.5 0.8 %copy.6 = bf16[256,1024]{1,0:T(8,128)(2,1)} copy(bf16[256,1024]{1,0:T(8,128)(2,1)S(1)} %shard_map.46) | data formatting | bytes 1048576
Async XLA Ops:
  0.0 1.6 %copy-start = (bf16[1024,1024]{1,0:T(8,128)(2,1)S(1)}, bf16[1024,1024]{1,0:T(8,128)(2,1)}, u32[]{:S(2)}) copy-start(bf16[1024,1024]{1,0:T(8,128)(2,1)} %w_hbm.1) | copy-start | bytes 6291460
  1.6 1.0 %copy-start.1 = (bf16[256,1024]{1,0:T(8,128)(2,1)S(1)}, bf16[256,1024]{1,0:T(8,128)(2,1)}, u32[]{:S(2)}) copy-start(bf16[256,1024]{1,0:T(8,128)(2,1)} %q_hbm.1) | copy-start | bytes 1572868
  2.6 1.0 %copy-start.2 = (bf16[256,1024]{1,0:T(8,128)(2,1)S(1)}, bf16[256,1024]{1,0:T(8,128)(2,1)}, u32[]{:S(2)}) copy-start(bf16[256,1024]{1,0:T(8,128)(2,1)} %k_hbm.1) | copy-start | bytes 1572868
  3.7 1.0 %copy-start.3 = (bf16[256,1024]{1,0:T(8,128)(2,1)S(1)}, bf16[256,1024]{1,0:T(8,128)(2,1)}, u32[]{:S(2)}) copy-start(bf16[256,1024]{1,0:T(8,128)(2,1)} %v_hbm.1) | copy-start | bytes 1572868
where the time goes:
time: 56.5 us; the launch traced here: 56.3 us
  Pallas kernels  50.8 us (90%)
  local copies, waits for them, and re-layouts  5.51 us (10%)
    pallas_call x1, Pallas kernels, local(): pl.pallas_call(kernel, out_shape=jax.ShapeDtypeStruct((ROWS, D), BF), in_...  50.8 us
    unnamed x9, local copies, waits for them, and re-layouts  5.51 us

commit v1 on v0

--- a/solution.py
+++ b/solution.py
@@ -73,16 +73,16 @@
 
 
 def kernel(q_hbm, k_hbm, v_hbm, w_hbm, out_ref, *scratch):
-    (own, qp, kx, vx, wv, st4, r4, z4s, z5s, z6s, z4r, z5r, z6r, cos, cor, s2, r2, s3, r3, ab, ret, acc, rep,
+    (own, qp, kx, vx, wv, st4, r4, z4s, z5s, z6s, z4r, z5r, z6r, cos, cor, s2, r2, s3, r3, ab, ret, acc, rep, held, kv1, k0s, v0s,
      own_sem, pair_sem, w_sem, e1s, e1r, nats, natr, rels, relr, s2s, s2r, s3s, s3r, a2as, a2ar, zs, zr, cs, cr,
-     rs, rr, self_sem) = scratch
+     rs, rr, self_sem, plane_sem, z_sem) = scratch
     b, s = lax.axis_index("batch"), lax.axis_index("seq")
     h, x, z, p = s % 2, (s // 2) % 4, s // 8, s // 2
     me8 = s % 8
     partner = (b, p * 2 + 1 - h)
 
     def pair(index):
-        return (b, ((index + 32) % 32) * 2 + h)
+        return (b, index * 2 + h)
 
     def in_plane(x2):
         return (b, z * 8 + x2 * 2 + h)
@@ -111,12 +111,26 @@
     def received(dst, ssem, rsem):
         remote(dst, dst, ssem, rsem, partner).wait_recv()
 
+    def signal(sem, target):
+        pl.semaphore_signal(sem, inc=1, device_id=target, device_id_type=MESH)
+
+    def signal_z(sem, far):
+        @pl.when(z >= far)
+        def _():
+            signal(sem, along_z(z - far))
+
+        @pl.when(z < 8 - far)
+        def _():
+            signal(sem, along_z(z + far))
+
+    def count_z(far):
+        return jnp.where(z >= far, 1, 0) + jnp.where(z < 8 - far, 1, 0)
+
     barrier = pltpu.get_barrier_semaphore()
-    targets = [(b, z * 8 + (me8 + j) % 8) for j in range(1, 8)]
-    targets += [along_z((z + j) % 8) for j in range(1, 8)]
-    targets += [pair(p + 1), pair(p - 1)]
-    for target in targets:
-        pl.semaphore_signal(barrier, inc=1, device_id=target, device_id_type=MESH)
+    signal(barrier, partner)
+    for j in range(1, 4):
+        signal(barrier, in_plane((x + j) % 4))
+    signal_z(barrier, 1)
 
     inputs = (q_hbm, k_hbm, v_hbm)
     own_copies = [pltpu.make_async_copy(inputs[i], own.at[i], own_sem.at[i]) for i in range(3)]
@@ -145,22 +159,6 @@
     w_copy = pltpu.make_async_copy(w_hbm, wv, w_sem)
     w_copy.start()
 
-    for i in range(3):
-        own_copies[i].wait()
-        coarse = own[i]
-        for _ in range(4):
-            coarse = coarsen(coarse)
-        for hp in range(8):
-            st4[(hp % 4) * 2 + hp // 4, i] = coarse[:, hp * LANES : (hp + 1) * LANES]
-
-    pl.semaphore_wait(barrier, len(targets))
-
-    for j in range(1, 8):
-        t = (me8 + j) % 8
-        send(st4.at[t], r4.at[:, pl.ds(pl.multiple_of(me8 * 16, 16), 16)], a2as.at[t], a2ar.at[me8], (b, z * 8 + t))
-    self_copy = pltpu.make_async_copy(st4.at[me8], r4.at[:, pl.ds(pl.multiple_of(me8 * 16, 16), 16)], self_sem)
-    self_copy.start()
-
     def exchange(c, i):
         send(
             inputs[i].at[:, theirs(c)],
@@ -173,35 +171,108 @@
     def exchanged(c, i):
         received(pair_refs[i].at[c, at(offsets[i] + ROWS * (1 - h), ROWS)], e1s.at[c, i], e1r.at[c, i])
 
-    for c, i in ((0, 1), (0, 2), (1, 1), (1, 2), (0, 0), (2, 1), (2, 2), (1, 0), (3, 1), (3, 2), (2, 0), (3, 0)):
-        exchange(c, i)
-
-    native_target = pair(p - 1 + 2 * h)
-    relay_target = pair(p + 1 - 2 * h)
-    for c in range(CHUNKS):
-        for i in (1, 2):
+    def level4():
+        for i in range(3):
+            own_copies[i].wait()
+        coarse = [own[i] for i in range(3)]
+        for _ in range(4):
+            coarse = [coarsen(level) for level in coarse]
+        for i in range(3):
+            for hp in range(8):
+                st4[(hp % 4) * 2 + hp // 4, i] = coarse[i][:, hp * LANES : (hp + 1) * LANES]
+        pl.semaphore_wait(plane_sem, 1)
+        for j in range(1, 8):
+            t = (me8 + j) % 8
             send(
-                inputs[i].at[at(BLOCK * h, BLOCK), mine(c)],
-                pair_refs[i].at[c, at(640 * (1 - h), BLOCK)],
-                nats.at[c, i - 1],
-                natr.at[c, i - 1],
-                native_target,
+                st4.at[t], r4.at[:, pl.ds(pl.multiple_of(me8 * 16, 16), 16)], a2as.at[t], a2ar.at[me8], (b, z * 8 + t)
             )
+        self_copy.start()
+
+    self_copy = pltpu.make_async_copy(st4.at[me8], r4.at[:, pl.ds(pl.multiple_of(me8 * 16, 16), 16)], self_sem)
+
+    native_pair, relay_pair = p - 1 + 2 * h, p + 1 - 2 * h
+    native_there = (native_pair >= 0) & (native_pair <= 31)
+    relay_there = (relay_pair >= 0) & (relay_pair <= 31)
+
+    def native_rim(c, i):
+        return remote(
+            inputs[i].at[at(BLOCK * h, BLOCK), mine(c)],
+            pair_refs[i].at[c, at(640 * (1 - h), BLOCK)],
+            nats.at[c, i - 1],
+            natr.at[c, i - 1],
+            pair(native_pair),
+        )
+
+    def relay_rim(c, i):
+        return remote(
+            pair_refs[i].at[c, at(BLOCK * (4 - 3 * h), BLOCK)],
+            pair_refs[i].at[c, at(640 * h, BLOCK)],
+            rels.at[c, i - 1],
+            relr.at[c, i - 1],
+            pair(relay_pair),
+        )
+
+    def native_rims():
+        @pl.when(native_there)
+        def _():
+            for c in range(CHUNKS):
+                for i in (1, 2):
+                    native_rim(c, i).start()
+
+    def rims_received(c):
+        @pl.when(relay_there)
+        def _():
+            for i in (1, 2):
+                received(pair_refs[i].at[c, at(640 * (1 - h), BLOCK)], nats.at[c, i - 1], natr.at[c, i - 1])
+
+        @pl.when(native_there)
+        def _():
+            for i in (1, 2):
+                received(pair_refs[i].at[c, at(640 * h, BLOCK)], rels.at[c, i - 1], relr.at[c, i - 1])
+
+    def rims_sent():
+        @pl.when(native_there)
+        def _():
+            for c in range(CHUNKS):
+                for i in (1, 2):
+                    native_rim(c, i).wait_send()
+
+        @pl.when(relay_there)
+        def _():
+            for c in range(CHUNKS):
+                for i in (1, 2):
+                    relay_rim(c, i).wait_send()
+
+    def no_rims():
+        @pl.when(p == 0)
+        def _():
+            for ref in (kx, vx):
+                ref[:, :BLOCK] = jnp.zeros((CHUNKS, BLOCK, LANES), BF)
+
+        @pl.when(p == 31)
+        def _():
+            for ref in (kx, vx):
+                ref[:, 640:] = jnp.zeros((CHUNKS, BLOCK, LANES), BF)
 
     def spread(c):
         for i in (1, 2):
             pair_copies[c * 3 + i].wait()
             exchanged(c, i)
-            send(
-                pair_refs[i].at[c, at(BLOCK * (4 - 3 * h), BLOCK)],
-                pair_refs[i].at[c, at(640 * h, BLOCK)],
-                rels.at[c, i - 1],
-                relr.at[c, i - 1],
-                relay_target,
-            )
-            level2 = coarsen(coarsen(pair_refs[i][c, BLOCK : BLOCK + 512]))
-            s2[c, i - 1] = level2
-            s3[c, i - 1] = coarsen(level2)
+
+        @pl.when(relay_there)
+        def _():
+            for i in (1, 2):
+                relay_rim(c, i).start()
+
+        fine = jnp.concatenate([kx[c, BLOCK : BLOCK + 512], vx[c, BLOCK : BLOCK + 512]], axis=1)
+        level1 = coarsen(fine)
+        level2 = coarsen(level1)
+        level3 = coarsen(level2)
+        for i in range(2):
+            side = slice(LANES * i, LANES * i + LANES)
+            s2[c, i] = level2[:, side]
+            s3[c, i] = level3[:, side]
+            kv1[c, i] = level1[:, side]
         send(s2.at[c], r2.at[c], s2s.at[c], s2r.at[c], in_plane(flip(x, 1)))
         for k in (0, 1):
             send(
@@ -219,6 +290,7 @@
             z4s[i - 1] = level4
             z5s[i - 1] = level5
             z6s[i - 1] = coarsen(level5)
+        pl.semaphore_wait(z_sem.at[2], count_z(4))
         send(z4s, z4r, zs.at[0], zr.at[0], along_z(flip(z, 1)))
         for k in range(2):
             send(z5s, z5r.at[:, pl.ds(64 * k, 64)], zs.at[1 + k], zr.at[1 + k], along_z(flip(z, 2 + k)))
@@ -259,32 +331,32 @@
             x2 = (x + j) % 4
             received(cor.at[x2], cs.at[x2], cr.at[x2])
 
-    def compute(c):
+    def windows(c, deferred):
         pair_copies[c * 3].wait()
         exchanged(c, 0)
+        rims_received(c)
+        received(r2.at[c], s2s.at[c], s2r.at[c])
+        for k in (0, 1):
+            received(r3.at[c, :, pl.ds(64 * k, 64)], s3s.at[c, k], s3r.at[c, k])
         q0 = qp[c]
         q1 = coarsen(q0)
         q2 = coarsen(q1)
         q3 = coarsen(q2)
-        for k in (0, 1):
-            received(r3.at[c, :, pl.ds(64 * k, 64)], s3s.at[c, k], s3r.at[c, k])
-        level = tuple(cor[c, i] for i in range(3))
-        level = merge(repeated(level), attend(q3, split_keys(r3[c, 0]), split_values(r3[c, 1])))
-        received(r2.at[c], s2s.at[c], s2r.at[c])
+        level = attend(q3, split_keys(r3[c, 0]), split_values(r3[c, 1]))
+        if not deferred:
+            level = merge(repeated(tuple(cor[c, i] for i in range(3))), level)
         level = merge(repeated(level), attend(q2, split_keys(r2[c, 0]), split_values(r2[c, 1])))
-        k1 = split_keys(coarsen(kx[c, BLOCK : BLOCK + 512]))
-        v1 = split_values(coarsen(vx[c, BLOCK : BLOCK + 512]))
+        k1 = split_keys(kv1[c, 0])
+        v1 = split_values(kv1[c, 1])
         parts = []
         for block in (0, 1):
             other = slice(128 * (1 - block), 128 * (2 - block))
             parts.append(attend(q1[128 * block : 128 * block + 128], [k[other] for k in k1], [v[other] for v in v1]))
         fine = tuple(jnp.concatenate([part[i] for part in parts], axis=0) for i in range(3))
         level = repeated(merge(repeated(level), fine))
-        for i in (1, 2):
-            received(pair_refs[i].at[c, at(640 * (1 - h), BLOCK)], nats.at[c, i - 1], natr.at[c, i - 1])
-            received(pair_refs[i].at[c, at(640 * h, BLOCK)], rels.at[c, i - 1], relr.at[c, i - 1])
-        k0 = split_keys(kx[c])
-        v0 = split_values(vx[c])
+        for head, (k0, v0) in enumerate(zip(split_keys(kx[c]), split_values(vx[c]))):
+            k0s[head] = k0
+            v0s[head] = v0
         for block in range(4):
             window = slice(128 * block, 128 * block + 384)
             rows = slice(128 * block, 128 * block + 128)
@@ -293,22 +365,59 @@
                 masks = ((0, 128, p == 0),)
             if block == 3:
                 masks = ((256, 384, p == 31),)
-            fine = attend(q0[rows], [k[window] for k in k0], [v[window] for v in v0], masks)
-            _, mass, summary = merge(tuple(a[rows] for a in level), fine)
+            fine = attend(q0[rows], [k0s[0, window], k0s[1, window]], [v0s[0, window], v0s[1, window]], masks)
+            merged = merge(tuple(a[rows] for a in level), fine)
+            if deferred:
+                for i in range(3):
+                    held[c, i, rows] = merged[i]
+            else:
+                ab[c, rows] = (merged[2] / merged[1]).astype(BF)
+
+    def late_merge(c):
+        for i in range(3):
+            level = cor[c, i]
+            for k in range(16):
+                rep[i, pl.ds(k, 32, stride=16), :] = level
+        for block in range(4):
+            rows = slice(128 * block, 128 * block + 128)
+            _, mass, summary = merge(tuple(rep[i, rows] for i in range(3)), tuple(held[c, i, rows] for i in range(3)))
             ab[c, rows] = (summary / mass).astype(BF)
+
+    def give_back(c):
         send(ab.at[c, at(ROWS * (1 - h), ROWS)], ret.at[c], rs.at[c], rr.at[c], partner)
 
+    no_rims()
+    pl.semaphore_wait(barrier, 4 + count_z(1))
+    signal(plane_sem, partner)
+    signal_z(z_sem.at[0], 1)
+    exchange(0, 1)
+    exchange(0, 2)
+    level4()
+    for c, i in ((1, 1), (1, 2), (0, 0), (2, 1), (2, 2), (1, 0), (3, 1), (3, 2), (2, 0), (3, 0)):
+        exchange(c, i)
+    pl.semaphore_wait(z_sem.at[0], count_z(1))
+    signal_z(z_sem.at[1], 2)
+    native_rims()
     spread(0)
+    pl.semaphore_wait(z_sem.at[1], count_z(2))
+    signal_z(z_sem.at[2], 4)
+    spread(1)
     coarse_spread()
-    spread(1)
+    windows(0, True)
+    spread(2)
+    windows(1, True)
     coarse_attend()
-    spread(2)
+    spread(3)
+    windows(2, True)
     coarse_received()
-    compute(0)
-    spread(3)
-    compute(1)
-    compute(2)
-    compute(3)
+    late_merge(0)
+    give_back(0)
+    late_merge(1)
+    give_back(1)
+    late_merge(2)
+    give_back(2)
+    windows(3, False)
+    give_back(3)
 
     w_copy.wait()
     for c in range(CHUNKS):
@@ -328,6 +437,7 @@
             out_ref[...] = (acc[...] + part).astype(BF)
     for copy in sent:
         copy.wait_send()
+    rims_sent()
 
 
 def local(queries, keys, values, out_weight):
@@ -357,6 +467,10 @@
         vmem((CHUNKS, ROWS, LANES), BF),
         vmem((ROWS, D), F32),
         vmem((3, 512, LANES), F32),
+        vmem((CHUNKS, 3, 512, LANES), F32),
+        vmem((CHUNKS, 2, 256, LANES), BF),
+        vmem((2, 768, LANES), BF),
+        vmem((2, 768, 2 * LANES), BF),
         dma((3,)),
         dma((CHUNKS, 3)),
         dma,
@@ -379,6 +493,8 @@
         dma((CHUNKS,)),
         dma((CHUNKS,)),
         dma,
+        pltpu.SemaphoreType.REGULAR,
+        pltpu.SemaphoreType.REGULAR((3,)),
     ]
     anywhere = pl.BlockSpec(memory_space=pl.ANY)
     return pl.pallas_call(
@@ -388,7 +504,7 @@
         out_specs=pl.BlockSpec(memory_space=pltpu.VMEM),
         scratch_shapes=scratch,
         compiler_params=pltpu.CompilerParams(
-            collective_id=0, has_side_effects=True, vmem_limit_bytes=40 << 20
+            collective_id=0, has_side_effects=True, vmem_limit_bytes=56 << 20
         ),
         cost_estimate=pl.CostEstimate(flops=1 << 30, bytes_accessed=4 << 20, transcendentals=1 << 21),
     )(queries, keys, values, out_weight)

time: 56.5 us -> 45.3 us (0.80)
  Pallas kernels: 50.8 us -> 43.3 us
  local copies, waits for them, and re-layouts: 5.51 us -> 1.87 us
    pallas_call x1, Pallas kernels: 50.8 us -> 43.3 us  [local(): pl.pallas_call(kernel, out_shape=jax.ShapeDtypeStruct((ROWS, D), BF), in_...]
    unnamed x9 -> x1, local copies, waits for them, and re-layouts: 5.51 us -> 1.87 us
where the time goes in v1:
time: 45.3 us; the launch traced here: 45.2 us
  Pallas kernels  43.3 us (96%)
  local copies, waits for them, and re-layouts  1.87 us (4%)
    pallas_call x1, Pallas kernels, local(): pl.pallas_call(kernel, out_shape=jax.ShapeDtypeStruct((ROWS, D), BF), in_...  43.3 us
    unnamed x1, local copies, waits for them, and re-layouts  1.87 us

profile of v1, /device:TPU:2, one launch (start us, length us, event | category | flops | bytes accessed | tf_op | source)
XLA Modules:
  0.0 45.2 jit_solution(4224103814682022267)
XLA Ops:
  0.0 43.3 %shard_map.46 = bf16[256,1024]{1,0:T(8,128)(2,1)} custom-call(bf16[256,1024]{1,0:T(8,128)(2,1)} %q_hbm.1, bf16[256,1024]{1,0:T(8,128)(2,1)} %k_hbm.1, bf16[256,1024]{1,0:T(8,128)(2,1)} %v_hbm.1, bf16[1024,1024]{1,0:T(8,128)(2,1)} %w_hbm.1), custom_call_target="tpu_custom_call" | custom-call | flops 1073741824 | bytes 4194304 | tf_op jit(solution)/shard_map/pallas_call | solution.py:500
  43.3 1.9 %copy.6 = bf16[256,1024]{1,0:T(8,128)(2,1)} copy(bf16[256,1024]{1,0:T(8,128)(2,1)} %shard_map.46) | data formatting | bytes 1048576

commit v2 on v1

--- a/solution.py
+++ b/solution.py
@@ -49,21 +49,43 @@
     )
 
 
-def attend(q, keys, values, masks=()):
+def scored(q, keys, values, hidden=None):
+    scores = []
+    for k in keys():
+        s = lax.dot_general(q(), k, (((1,), (1,)), ((), ())), preferred_element_type=F32)
+        if hidden is not None:
+            first, last, masked = hidden
+            parts = [s[:, :first], jnp.where(masked, MASKED, s[:, first:last]), s[:, last:]]
+            s = jnp.concatenate([part for part in parts if part.shape[1]], axis=1)
+        scores.append(s)
+    return scores
+
+
+def weighted(scores):
     weights, peaks = [], []
-    for k in keys:
-        s = lax.dot_general(q, k, (((1,), (1,)), ((), ())), preferred_element_type=F32)
-        for first, last, hidden in masks:
-            parts = [s[:, :first], jnp.where(hidden, MASKED, s[:, first:last]), s[:, last:]]
-            s = jnp.concatenate([part for part in parts if part.shape[1]], axis=1)
+    for s in scores:
         peak = jnp.max(s, axis=1, keepdims=True)
         weights.append(jnp.exp2((s - peak) * FACTOR).astype(BF))
         peaks.append(peak * FACTOR)
-    total = jnp.dot(
-        jnp.concatenate(weights, axis=1), jnp.concatenate(values, axis=0), preferred_element_type=F32
-    )
-    peak = jnp.where(low_lanes(q.shape[0]), peaks[0], peaks[1])
+    return jnp.concatenate(weights, axis=1), jnp.where(low_lanes(scores[0].shape[0]), peaks[0], peaks[1])
+
+
+def summed(weights, peak, values):
+    total = jnp.dot(weights, jnp.concatenate(values, axis=0), preferred_element_type=F32)
     return peak, total[:, LANES:], total[:, :LANES]
+
+
+def attend(units, done=None):
+    scores, weights, results = {}, {}, []
+    for step in range(len(units) + 3):
+        if step < len(units):
+            scores[step] = scored(*units[step])
+        if 0 <= step - 2 < len(units):
+            weights[step - 2] = weighted(scores.pop(step - 2))
+        if step >= 3:
+            result = summed(*weights.pop(step - 3), units[step - 3][2]())
+            results.append(result if done is None else done(step - 3, result))
+    return results
 
 
 def merge(a, b):
@@ -180,6 +202,8 @@
         for i in range(3):
             for hp in range(8):
                 st4[(hp % 4) * 2 + hp // 4, i] = coarse[i][:, hp * LANES : (hp + 1) * LANES]
+
+    def level4_spread():
         pl.semaphore_wait(plane_sem, 1)
         for j in range(1, 8):
             t = (me8 + j) % 8
@@ -212,12 +236,11 @@
             pair(relay_pair),
         )
 
-    def native_rims():
+    def native_rims(c):
         @pl.when(native_there)
         def _():
-            for c in range(CHUNKS):
-                for i in (1, 2):
-                    native_rim(c, i).start()
+            for i in (1, 2):
+                native_rim(c, i).start()
 
     def rims_received(c):
         @pl.when(relay_there)
@@ -290,12 +313,26 @@
             z4s[i - 1] = level4
             z5s[i - 1] = level5
             z6s[i - 1] = coarsen(level5)
-        pl.semaphore_wait(z_sem.at[2], count_z(4))
         send(z4s, z4r, zs.at[0], zr.at[0], along_z(flip(z, 1)))
         for k in range(2):
             send(z5s, z5r.at[:, pl.ds(64 * k, 64)], zs.at[1 + k], zr.at[1 + k], along_z(flip(z, 2 + k)))
-        for k in range(4):
-            send(z6s, z6r.at[:, pl.ds(32 * k, 32)], zs.at[3 + k], zr.at[3 + k], along_z(flip(z, 4 + k)))
+
+    def far_copies():
+        return [
+            remote(z6s, z6r.at[:, pl.ds(32 * k, 32)], zs.at[3 + k], zr.at[3 + k], along_z(flip(z, 4 + k)))
+            for k in range(4)
+        ]
+
+    def coarse_far():
+        pl.semaphore_wait(z_sem.at[2], 1)
+        for copy in far_copies():
+            copy.start()
+
+    def coarse_far_late_planes():
+        pl.when(z >= 4)(coarse_far)
+
+    def coarse_far_early_planes():
+        pl.when(z < 4)(coarse_far)
 
     def repeated(level):
         rows = level[0].shape[0]
@@ -313,9 +350,12 @@
         q4 = r4[0]
         q5 = coarsen(q4)
         q6 = coarsen(q5)
-        level = attend(q6, split_keys(z6r[0]), split_values(z6r[1]))
-        level = merge(repeated(level), attend(q5, split_keys(z5r[0]), split_values(z5r[1])))
-        level = merge(repeated(level), attend(q4, split_keys(z4r[0]), split_values(z4r[1])))
+        level, level5, level4 = attend([
+            (lambda q=q, r=r: q, lambda r=r: split_keys(r[0]), lambda r=r: split_values(r[1]))
+            for q, r in ((q6, z6r), (q5, z5r), (q4, z4r))
+        ])
+        level = merge(repeated(level), level5)
+        level = merge(repeated(level), level4)
         for i in range(3):
             for x2 in range(4):
                 cos[x2, i] = level[i][x2 * 32 : x2 * 32 + 32]
@@ -330,6 +370,9 @@
         for j in range(1, 4):
             x2 = (x + j) % 4
             received(cor.at[x2], cs.at[x2], cr.at[x2])
+
+    def give_back(c):
+        send(ab.at[c, at(ROWS * (1 - h), ROWS)], ret.at[c], rs.at[c], rr.at[c], partner)
 
     def windows(c, deferred):
         pair_copies[c * 3].wait()
@@ -342,36 +385,66 @@
         q1 = coarsen(q0)
         q2 = coarsen(q1)
         q3 = coarsen(q2)
-        level = attend(q3, split_keys(r3[c, 0]), split_values(r3[c, 1]))
-        if not deferred:
-            level = merge(repeated(tuple(cor[c, i] for i in range(3))), level)
-        level = merge(repeated(level), attend(q2, split_keys(r2[c, 0]), split_values(r2[c, 1])))
-        k1 = split_keys(kv1[c, 0])
-        v1 = split_values(kv1[c, 1])
-        parts = []
-        for block in (0, 1):
-            other = slice(128 * (1 - block), 128 * (2 - block))
-            parts.append(attend(q1[128 * block : 128 * block + 128], [k[other] for k in k1], [v[other] for v in v1]))
-        fine = tuple(jnp.concatenate([part[i] for part in parts], axis=0) for i in range(3))
-        level = repeated(merge(repeated(level), fine))
         for head, (k0, v0) in enumerate(zip(split_keys(kx[c]), split_values(vx[c]))):
             k0s[head] = k0
             v0s[head] = v0
-        for block in range(4):
-            window = slice(128 * block, 128 * block + 384)
-            rows = slice(128 * block, 128 * block + 128)
-            masks = ()
-            if block == 0:
-                masks = ((0, 128, p == 0),)
-            if block == 3:
-                masks = ((256, 384, p == 31),)
-            fine = attend(q0[rows], [k0s[0, window], k0s[1, window]], [v0s[0, window], v0s[1, window]], masks)
-            merged = merge(tuple(a[rows] for a in level), fine)
-            if deferred:
-                for i in range(3):
-                    held[c, i, rows] = merged[i]
+        k1 = split_keys(kv1[c, 0])
+        v1 = split_values(kv1[c, 1])
+
+        def block_of(unit):
+            return (2 * (1 - h), 2 * (1 - h) + 1, 2 * h, 2 * h + 1)[unit]
+
+        def fine_unit(unit):
+            block = block_of(unit)
+            start = BLOCK * block
+            hidden = ((0, 128, (p == 0) & (block == 0)), (256, 384, (p == 31) & (block == 3)))[unit % 2]
+            return (
+                lambda: qp[c, at(start, BLOCK)],
+                lambda: [k0s[0, at(start, 384)], k0s[1, at(start, 384)]],
+                lambda: [v0s[0, at(start, 384)], v0s[1, at(start, 384)]],
+                hidden,
+            )
+
+        def sibling_unit(block):
+            other = slice(128 * (1 - block), 128 * (2 - block))
+            return (
+                lambda: q1[128 * block : 128 * block + 128],
+                lambda: [k[other] for k in k1],
+                lambda: [v[other] for v in v1],
+            )
+
+        units = [
+            (lambda: q3, lambda: split_keys(r3[c, 0]), lambda: split_values(r3[c, 1])),
+            (lambda: q2, lambda: split_keys(r2[c, 0]), lambda: split_values(r2[c, 1])),
+            sibling_unit(0),
+            sibling_unit(1),
+        ] + [fine_unit(unit) for unit in range(4)]
+        state = {}
+
+        def done(index, result):
+            if index == 0:
+                if not deferred:
+                    result = merge(repeated(tuple(cor[c, i] for i in range(3))), result)
+                state["level"] = result
+            elif index == 1:
+                state["level"] = merge(repeated(state["level"]), result)
+            elif index == 2:
+                state["half"] = result
+            elif index == 3:
+                both = tuple(jnp.concatenate([state["half"][i], result[i]], axis=0) for i in range(3))
+                repeated(merge(repeated(state["level"]), both))
             else:
-                ab[c, rows] = (merged[2] / merged[1]).astype(BF)
+                rows = at(BLOCK * block_of(index - 4), BLOCK)
+                merged = merge(tuple(rep[i, rows] for i in range(3)), result)
+                if deferred:
+                    for i in range(3):
+                        held[c, i, rows] = merged[i]
+                else:
+                    ab[c, rows] = (merged[2] / merged[1]).astype(BF)
+                    if index == 5:
+                        give_back(c)
+
+        attend(units, done)
 
     def late_merge(c):
         for i in range(3):
@@ -383,31 +456,34 @@
             _, mass, summary = merge(tuple(rep[i, rows] for i in range(3)), tuple(held[c, i, rows] for i in range(3)))
             ab[c, rows] = (summary / mass).astype(BF)
 
-    def give_back(c):
-        send(ab.at[c, at(ROWS * (1 - h), ROWS)], ret.at[c], rs.at[c], rr.at[c], partner)
-
     no_rims()
+    level4()
     pl.semaphore_wait(barrier, 4 + count_z(1))
     signal(plane_sem, partner)
     signal_z(z_sem.at[0], 1)
     exchange(0, 1)
     exchange(0, 2)
-    level4()
-    for c, i in ((1, 1), (1, 2), (0, 0), (2, 1), (2, 2), (1, 0), (3, 1), (3, 2), (2, 0), (3, 0)):
+    level4_spread()
+    for c, i in ((1, 1), (1, 2), (0, 0), (2, 1), (2, 2), (3, 1), (3, 2), (1, 0), (2, 0), (3, 0)):
         exchange(c, i)
     pl.semaphore_wait(z_sem.at[0], count_z(1))
     signal_z(z_sem.at[1], 2)
-    native_rims()
+    native_rims(0)
     spread(0)
+    native_rims(1)
     pl.semaphore_wait(z_sem.at[1], count_z(2))
     signal_z(z_sem.at[2], 4)
+    coarse_spread()
+    coarse_far_late_planes()
     spread(1)
-    coarse_spread()
+    native_rims(2)
     windows(0, True)
+    coarse_far_early_planes()
     spread(2)
+    coarse_attend()
+    native_rims(3)
+    spread(3)
     windows(1, True)
-    coarse_attend()
-    spread(3)
     windows(2, True)
     coarse_received()
     late_merge(0)
@@ -417,7 +493,11 @@
     late_merge(2)
     give_back(2)
     windows(3, False)
-    give_back(3)
+
+    def finish():
+        for copy in sent + far_copies():
+            copy.wait_send()
+        rims_sent()
 
     w_copy.wait()
     for c in range(CHUNKS):
@@ -430,14 +510,15 @@
             acc[...] += part
     for c in range(CHUNKS):
         received(ret.at[c], rs.at[c], rr.at[c])
-        part = jnp.dot(ret[c], wv[at(HALF * (1 - h) + LANES * c, LANES)], preferred_element_type=F32)
+        weight = wv[at(HALF * (1 - h) + LANES * c, LANES)]
         if c < CHUNKS - 1:
-            acc[...] += part
+            acc[...] += jnp.dot(ret[c], weight, preferred_element_type=F32)
         else:
-            out_ref[...] = (acc[...] + part).astype(BF)
-    for copy in sent:
-        copy.wait_send()
-    rims_sent()
+            for i in range(4):
+                rows = slice(64 * i, 64 * i + 64)
+                part = jnp.dot(ret[c, rows], weight, preferred_element_type=F32)
+                out_ref[rows] = (acc[rows] + part).astype(BF)
+    finish()
 
 
 def local(queries, keys, values, out_weight):
@@ -499,7 +580,7 @@
     anywhere = pl.BlockSpec(memory_space=pl.ANY)
     return pl.pallas_call(
         kernel,
-        out_shape=jax.ShapeDtypeStruct((ROWS, D), BF),
+        out_shape=pltpu.VMEM((ROWS, D), BF),
         in_specs=[anywhere] * 4,
         out_specs=pl.BlockSpec(memory_space=pltpu.VMEM),
         scratch_shapes=scratch,

time: 45.3 us -> 38.1 us (0.84); the launches traced: 45.2 us -> 37.4 us
  Pallas kernels: 43.3 us -> 36.6 us
  local copies, waits for them, and re-layouts: 1.87 us -> 0.8 us
    pallas_call x1, Pallas kernels: 43.3 us -> 36.6 us  [local(): pl.pallas_call(kernel, out_shape=pltpu.VMEM((ROWS, D), BF), in_specs=[any...]
    unnamed x1, local copies, waits for them, and re-layouts: 1.87 us -> 0.8 us
where the time goes in v2:
time: 38.1 us; the launch traced here: 37.4 us
  Pallas kernels  36.6 us (96%)
  local copies, waits for them, and re-layouts  0.8 us (2%)
    pallas_call x1, Pallas kernels, local(): pl.pallas_call(kernel, out_shape=pltpu.VMEM((ROWS, D), BF), in_specs=[any...  36.6 us
    unnamed x1, local copies, waits for them, and re-layouts  0.8 us

profile of v2, /device:TPU:2, one launch (start us, length us, event | category | flops | bytes accessed | tf_op | source)
XLA Modules:
  0.0 37.4 jit_solution(1524614208645643838)
XLA Ops:
  0.0 36.6 %shard_map.46 = bf16[256,1024]{1,0:T(8,128)(2,1)S(1)} custom-call(bf16[256,1024]{1,0:T(8,128)(2,1)} %q_hbm.1, bf16[256,1024]{1,0:T(8,128)(2,1)} %k_hbm.1, bf16[256,1024]{1,0:T(8,128)(2,1)} %v_hbm.1, bf16[1024,1024]{1,0:T(8,128)(2,1)} %w_hbm.1), custom_call_target="tpu_custom_call" | custom-call | flops 1073741824 | bytes 4194304 | tf_op jit(solution)/shard_map/pallas_call | solution.py:581
  36.6 0.8 %copy.6 = bf16[256,1024]{1,0:T(8,128)(2,1)} copy(bf16[256,1024]{1,0:T(8,128)(2,1)S(1)} %shard_map.46) | data formatting | bytes 1048576

commit v3 on v2

--- a/solution.py
+++ b/solution.py
@@ -136,23 +136,32 @@
     def signal(sem, target):
         pl.semaphore_signal(sem, inc=1, device_id=target, device_id_type=MESH)
 
-    def signal_z(sem, far):
+    def signal_up(sem, far):
+        @pl.when(z < 8 - far)
+        def _():
+            signal(sem, along_z(z + far))
+
+    def signal_down(sem, far):
         @pl.when(z >= far)
         def _():
             signal(sem, along_z(z - far))
 
+    def wait_up(sem, far):
+        @pl.when(z >= far)
+        def _():
+            pl.semaphore_wait(sem, 1)
+
+    def wait_down(sem, far):
         @pl.when(z < 8 - far)
         def _():
-            signal(sem, along_z(z + far))
-
-    def count_z(far):
-        return jnp.where(z >= far, 1, 0) + jnp.where(z < 8 - far, 1, 0)
+            pl.semaphore_wait(sem, 1)
 
     barrier = pltpu.get_barrier_semaphore()
     signal(barrier, partner)
     for j in range(1, 4):
         signal(barrier, in_plane((x + j) % 4))
-    signal_z(barrier, 1)
+    signal_up(barrier, 1)
+    signal_down(barrier, 1)
 
     inputs = (q_hbm, k_hbm, v_hbm)
     own_copies = [pltpu.make_async_copy(inputs[i], own.at[i], own_sem.at[i]) for i in range(3)]
@@ -181,14 +190,19 @@
     w_copy = pltpu.make_async_copy(w_hbm, wv, w_sem)
     w_copy.start()
 
-    def exchange(c, i):
-        send(
+    def exchange_copy(c, i):
+        return remote(
             inputs[i].at[:, theirs(c)],
             pair_refs[i].at[c, at(offsets[i] + ROWS * h, ROWS)],
             e1s.at[c, i],
             e1r.at[c, i],
             partner,
         )
+
+    def exchange(c, i):
+        copy = exchange_copy(c, i)
+        copy.start()
+        sent.append(copy)
 
     def exchanged(c, i):
         received(pair_refs[i].at[c, at(offsets[i] + ROWS * (1 - h), ROWS)], e1s.at[c, i], e1r.at[c, i])
@@ -313,9 +327,14 @@
             z4s[i - 1] = level4
             z5s[i - 1] = level5
             z6s[i - 1] = coarsen(level5)
-        send(z4s, z4r, zs.at[0], zr.at[0], along_z(flip(z, 1)))
-        for k in range(2):
-            send(z5s, z5r.at[:, pl.ds(64 * k, 64)], zs.at[1 + k], zr.at[1 + k], along_z(flip(z, 2 + k)))
+        for copy in near_copies():
+            copy.start()
+
+    def near_copies():
+        return [remote(z4s, z4r, zs.at[0], zr.at[0], along_z(flip(z, 1)))] + [
+            remote(z5s, z5r.at[:, pl.ds(64 * k, 64)], zs.at[1 + k], zr.at[1 + k], along_z(flip(z, 2 + k)))
+            for k in range(2)
+        ]
 
     def far_copies():
         return [
@@ -324,14 +343,19 @@
         ]
 
     def coarse_far():
-        pl.semaphore_wait(z_sem.at[2], 1)
         for copy in far_copies():
             copy.start()
 
-    def coarse_far_late_planes():
-        pl.when(z >= 4)(coarse_far)
+    def coarse_late_planes():
+        wait_up(z_sem.at[2], 4)
+        coarse_spread()
+        coarse_far()
+
+    def coarse_early_planes():
+        coarse_spread()
 
     def coarse_far_early_planes():
+        wait_down(z_sem.at[5], 4)
         pl.when(z < 4)(coarse_far)
 
     def repeated(level):
@@ -446,39 +470,54 @@
 
         attend(units, done)
 
-    def late_merge(c):
+    def late_merge(c, side):
         for i in range(3):
-            level = cor[c, i]
+            level = cor[c, i, pl.ds(pl.multiple_of(16 * side, 16), 16)]
             for k in range(16):
-                rep[i, pl.ds(k, 32, stride=16), :] = level
-        for block in range(4):
-            rows = slice(128 * block, 128 * block + 128)
-            _, mass, summary = merge(tuple(rep[i, rows] for i in range(3)), tuple(held[c, i, rows] for i in range(3)))
+                rep[i, pl.ds(k, 16, stride=16), :] = level
+        for block in range(2):
+            here = slice(BLOCK * block, BLOCK * block + BLOCK)
+            rows = at(ROWS * side + BLOCK * block, BLOCK)
+            _, mass, summary = merge(tuple(rep[i, here] for i in range(3)), tuple(held[c, i, rows] for i in range(3)))
             ab[c, rows] = (summary / mass).astype(BF)
 
+    def meet_next_planes():
+        wait_up(z_sem.at[0], 1)
+        wait_down(z_sem.at[3], 1)
+        signal_up(z_sem.at[1], 2)
+        signal_down(z_sem.at[4], 2)
+
+    def meet_far_planes():
+        wait_up(z_sem.at[1], 2)
+        wait_down(z_sem.at[4], 2)
+        signal_up(z_sem.at[2], 4)
+        signal_down(z_sem.at[5], 4)
+
     no_rims()
+    pl.semaphore_wait(barrier, 4 + jnp.where(z >= 1, 1, 0) + jnp.where(z < 7, 1, 0))
+    signal(plane_sem, partner)
+    signal_up(z_sem.at[0], 1)
+    signal_down(z_sem.at[3], 1)
+    exchange(0, 1)
+    first_values = exchange_copy(0, 2)
+    sent.append(first_values)
+    pl.when(z < 4)(first_values.start)
     level4()
-    pl.semaphore_wait(barrier, 4 + count_z(1))
-    signal(plane_sem, partner)
-    signal_z(z_sem.at[0], 1)
-    exchange(0, 1)
-    exchange(0, 2)
     level4_spread()
+    pl.when(z >= 4)(first_values.start)
     for c, i in ((1, 1), (1, 2), (0, 0), (2, 1), (2, 2), (3, 1), (3, 2), (1, 0), (2, 0), (3, 0)):
         exchange(c, i)
-    pl.semaphore_wait(z_sem.at[0], count_z(1))
-    signal_z(z_sem.at[1], 2)
+    meet_next_planes()
     native_rims(0)
+    meet_far_planes()
+    pl.when(z >= 4)(coarse_late_planes)
     spread(0)
     native_rims(1)
-    pl.semaphore_wait(z_sem.at[1], count_z(2))
-    signal_z(z_sem.at[2], 4)
-    coarse_spread()
-    coarse_far_late_planes()
+    pl.when(z < 4)(coarse_early_planes)
     spread(1)
     native_rims(2)
+    coarse_far_early_planes()
     windows(0, True)
-    coarse_far_early_planes()
     spread(2)
     coarse_attend()
     native_rims(3)
@@ -486,16 +525,19 @@
     windows(1, True)
     windows(2, True)
     coarse_received()
-    late_merge(0)
+    late_merge(0, 1 - h)
     give_back(0)
-    late_merge(1)
+    late_merge(1, 1 - h)
     give_back(1)
-    late_merge(2)
+    late_merge(2, 1 - h)
     give_back(2)
     windows(3, False)
+    late_merge(0, h)
+    late_merge(1, h)
+    late_merge(2, h)
 
     def finish():
-        for copy in sent + far_copies():
+        for copy in sent + near_copies() + far_copies():
             copy.wait_send()
         rims_sent()
 
@@ -575,7 +617,7 @@
         dma((CHUNKS,)),
         dma,
         pltpu.SemaphoreType.REGULAR,
-        pltpu.SemaphoreType.REGULAR((3,)),
+        pltpu.SemaphoreType.REGULAR((6,)),
     ]
     anywhere = pl.BlockSpec(memory_space=pl.ANY)
     return pl.pallas_call(

time: 38.1 us -> 37.6 us (0.987)
  no operation moved by 1% of the time
where the time goes in v3:
time: 37.6 us; the launch traced here: 37.2 us
  Pallas kernels  36.4 us (97%)
  local copies, waits for them, and re-layouts  0.8 us (2%)
    pallas_call x1, Pallas kernels, local(): pl.pallas_call(kernel, out_shape=pltpu.VMEM((ROWS, D), BF), in_specs=[any...  36.4 us
    unnamed x1, local copies, waits for them, and re-layouts  0.8 us

profile of v3, /device:TPU:2, one launch (start us, length us, event | category | flops | bytes accessed | tf_op | source)
XLA Modules:
  0.0 37.2 jit_solution(15193732559665457050)
XLA Ops:
  0.0 36.4 %shard_map.46 = bf16[256,1024]{1,0:T(8,128)(2,1)S(1)} custom-call(bf16[256,1024]{1,0:T(8,128)(2,1)} %q_hbm.1, bf16[256,1024]{1,0:T(8,128)(2,1)} %k_hbm.1, bf16[256,1024]{1,0:T(8,128)(2,1)} %v_hbm.1, bf16[1024,1024]{1,0:T(8,128)(2,1)} %w_hbm.1), custom_call_target="tpu_custom_call" | custom-call | flops 1073741824 | bytes 4194304 | tf_op jit(solution)/shard_map/pallas_call | solution.py:623
  36.4 0.8 %copy.6 = bf16[256,1024]{1,0:T(8,128)(2,1)} copy(bf16[256,1024]{1,0:T(8,128)(2,1)S(1)} %shard_map.46) | data formatting | bytes 1048576
